TPU v7x, 768 devices: a whole 4x8x12 slice. The times are simulated.
768 devices in a mesh: space: 192 (over x, z, y_hi, core), morder: 4 (over y_lo).
Axes of the slice: x: 4, y: 8 (y_hi: 2, y_lo: 4; y = y_hi * 4 + y_lo), z: 12, core: 2. Of those that a mesh axis runs over, the one named last changes fastest.
Arguments:
- nodes: bfloat16 [24576, 49, 128], P('space', None, 'morder'), may hold values from -6 to 6
- ghost_send: int32 [24576], P('space'), may hold values from 0 to 127, as said below
- edge_src: int32 [24576], P('space'), may hold values from 0 to 255
- edge_dst: int32 [24576], P('space'), may hold values from 0 to 127
- wigner: bfloat16 [24576, 29, 49], P('space'), may hold values from -6 to 6
- envelope: float32 [24576], P('space'), may hold values from 0.1 to 1
- w_zero: bfloat16 [896, 896], replicated, may hold values from -0.1875 to 0.1875
- w_one_real: bfloat16 [768, 768], replicated, may hold values from -0.15625 to 0.15625
- w_one_imag: bfloat16 [768, 768], replicated, may hold values from -0.15625 to 0.15625
- w_two_real: bfloat16 [640, 640], replicated, may hold values from -0.15625 to 0.15625
- w_two_imag: bfloat16 [640, 640], replicated, may hold values from -0.15625 to 0.15625
- cotangent: bfloat16 [24576, 49, 128], P('space', None, 'morder'), may hold values from -6 to 6
Outputs:
- updated: bfloat16 [24576, 49, 128], P('space', None, 'morder')
- node_grad: bfloat16 [24576, 49, 128], P('space', None, 'morder')
Inputs may be any that keep to these rules, and one draw needn't show every extreme that they name: `ghost_send`: indices of atoms of the sending domain itself; the 128 entries of one domain are all different. `edge_src`: indices into the domain's extended list: own atoms, then lower ghosts, then upper ghosts. `edge_dst`: indices of the domain's own atoms.
All inputs are finite; a program needn't handle non-finite values.
Results may differ from a plain program's by a relative error of at most 0.0051.
Values may be sent and summed in bfloat16 or wider, within the bound.
A program may use at most 64 MiB of HBM per device.

v0:
```python
import functools

import jax
import jax.numpy as jnp
from jax import lax
from jax.experimental import pallas as pl
from jax.experimental.pallas import tpu as pltpu
from jax.sharding import PartitionSpec as P

F32, BF16 = jnp.float32, jnp.bfloat16
LANES = 128
TOP = 25
NODE = 49
EDGE = 29
WIDE = 1024
PARTS = ((0, 7), (7, 6), (13, 6), (19, 5), (24, 5))


def degree_rows(degree):
    rows = [degree]
    if degree >= 1:
        rows += [6 + degree, 12 + degree]
    if degree >= 2:
        rows += [17 + degree, 22 + degree]
    return rows


def dot(a, b):
    return jnp.dot(a, b, preferred_element_type=F32)


def dot_t(a, b):
    return lax.dot_general(a, b, (((1,), (1,)), ((), ())), preferred_element_type=F32)


def one_hot(index_row, offset=0):
    rows = lax.broadcasted_iota(jnp.int32, (LANES, LANES), 0) + offset
    return jnp.where(rows == index_row, 1.0, 0.0).astype(F32)


def lane_low():
    return lax.broadcasted_iota(jnp.int32, (LANES, LANES), 1) < LANES // 2


def row_low():
    return lax.broadcasted_iota(jnp.int32, (LANES, LANES), 0) < LANES // 2


def rotate(rot_ref, load, store):
    for degree in range(7):
        columns = range(degree * degree, (degree + 1) * (degree + 1))
        for k in degree_rows(degree):
            total = None
            for n in columns:
                term = rot_ref[n, k : k + 1, :].astype(F32) * load(n)
                total = term if total is None else total + term
            store(k, total)


def rotate_back(rot_ref, load, store):
    for degree in range(7):
        for n in range(degree * degree, (degree + 1) * (degree + 1)):
            total = None
            for k in degree_rows(degree):
                term = rot_ref[n, k : k + 1, :].astype(F32) * load(k)
                total = term if total is None else total + term
            store(n, total)


def channel_rows(n, count=1):
    return slice(n * 32, (n + count) * 32)


def swap_blocks(blocks):
    group = lax.broadcasted_iota(jnp.int32, blocks[0].shape, 1) // 32
    low = group < 2
    a0 = jnp.where(low, blocks[0], pltpu.roll(blocks[2], 64, 1))
    a2 = jnp.where(low, pltpu.roll(blocks[0], 64, 1), blocks[2])
    a1 = jnp.where(low, blocks[1], pltpu.roll(blocks[3], 64, 1))
    a3 = jnp.where(low, pltpu.roll(blocks[1], 64, 1), blocks[3])
    even = (group % 2) == 0
    b0 = jnp.where(even, a0, pltpu.roll(a1, 32, 1))
    b1 = jnp.where(even, pltpu.roll(a0, 96, 1), a1)
    b2 = jnp.where(even, a2, pltpu.roll(a3, 32, 1))
    b3 = jnp.where(even, pltpu.roll(a2, 96, 1), a3)
    return [b0, b1, b2, b3]


def store_transposed(rows_ref, out_ref):
    for block in range(WIDE // LANES):
        piece = rows_ref[block * LANES : (block + 1) * LANES, :].T.astype(BF16)
        for part in range(4):
            out_ref[part, :, block * LANES : (block + 1) * LANES] = piece[part * 32 : (part + 1) * 32]


def load_transposed(in_ref, rows_ref):
    for block in range(WIDE // LANES):
        piece = jnp.concatenate(
            [in_ref[part, :, block * LANES : (block + 1) * LANES].astype(F32) for part in range(4)],
            axis=0,
        )
        rows_ref[block * LANES : (block + 1) * LANES, :] = piece.T


def prepare(nodes, cot, wig, send, dst, env, low, high, edge_out, rows, hot):
    match = one_hot(send[...])
    turned = pltpu.roll(match, 64, 1)
    side = lane_low()
    zero = jnp.zeros((LANES, LANES), F32)
    first = jnp.concatenate([jnp.where(side, match, zero), jnp.where(side, zero, match)], 1).astype(BF16)
    second = jnp.concatenate([jnp.where(side, zero, turned), jnp.where(side, turned, zero)], 1).astype(BF16)
    for n in range(0, TOP, 5):
        both = dot(nodes[channel_rows(n, 5)], first)
        count = min(5, NODE - TOP - n)
        other = dot(nodes[channel_rows(TOP + n, count)], second)
        if count < 5:
            other = jnp.concatenate([other, jnp.zeros(((5 - count) * 32, 256), F32)], 0)
        both = (both + other).astype(BF16)
        low[channel_rows(n, 5)] = both[:, :LANES]
        high[channel_rows(n, 5)] = both[:, LANES:]
    hot[...] = dot(cot[...], one_hot(dst[...]).astype(BF16))
    scale = env[...]

    def store(k, value):
        rows[channel_rows(k)] = value * scale

    rotate(wig, lambda n: hot[channel_rows(n)], store)
    rows[EDGE * 32 :] = jnp.zeros((WIDE - EDGE * 32, LANES), F32)
    store_transposed(rows, edge_out)


def lower_rotate(nodes, below, above, wig, src, edge_out, rows, hot):
    side = row_low()
    index = src[...]
    zero = jnp.zeros((LANES, LANES), F32)
    own = one_hot(index).astype(BF16)
    plain = one_hot(index, LANES)
    up = one_hot(index, LANES + 64)
    down = one_hot(index, 64)
    above_top = jnp.where(side, up, zero).astype(BF16)
    below_top = jnp.where(side, zero, down).astype(BF16)
    below_bottom = jnp.where(side, plain, zero).astype(BF16)
    above_bottom = jnp.where(side, zero, plain).astype(BF16)
    split = TOP * 32
    rest = (NODE - TOP) * 32
    hot[:split] = dot(nodes[:split], own) + dot(below[...], below_top) + dot(above[...], above_top)
    hot[split:] = (
        dot(nodes[split:], own) + dot(below[:rest], below_bottom) + dot(above[:rest], above_bottom)
    )

    def store(k, value):
        rows[channel_rows(k)] = value

    rotate(wig, lambda n: hot[channel_rows(n)], store)
    rows[EDGE * 32 :] = jnp.zeros((WIDE - EDGE * 32, LANES), F32)
    store_transposed(rows, edge_out)


def gather_channels(in_ref):
    result = []
    for group in range(WIDE // LANES):
        blocks = [in_ref[i, :, group * LANES : (group + 1) * LANES].astype(F32) for i in range(4)]
        result += swap_blocks(blocks)
    return result[:EDGE]


def spread_channels(blocks, out_ref):
    blocks = blocks + [jnp.zeros_like(blocks[0])] * 3
    for group in range(WIDE // LANES):
        for i, value in enumerate(swap_blocks(blocks[4 * group : 4 * group + 4])):
            out_ref[i, :, group * LANES : (group + 1) * LANES] = value.astype(BF16)


def map_edges(forward, in_ref, w_zero, w_one_real, w_one_imag, w_two_real, w_two_imag, out_ref):
    blocks = gather_channels(in_ref)
    product = dot if forward else dot_t

    def part(i):
        start, count = PARTS[i]
        return jnp.concatenate(blocks[start : start + count], 1).astype(BF16)

    results = []

    def put(value):
        results.extend(value[:, i * LANES : (i + 1) * LANES] for i in range(value.shape[1] // LANES))

    put(product(part(0), w_zero[...]))
    for first, real, imag in ((1, w_one_real, w_one_imag), (3, w_two_real, w_two_imag)):
        both = jnp.concatenate([part(first), part(first + 1)], 0)
        straight = product(both, real[...])
        crossed = product(both, imag[...])
        if forward:
            put(straight[:32] - crossed[32:])
            put(straight[32:] + crossed[:32])
        else:
            put(straight[:32] + crossed[32:])
            put(straight[32:] - crossed[:32])
    spread_channels(results, out_ref)


def finish_forward(nodes, edge_in, wig, env, dst, updated, rows, hot):
    load_transposed(edge_in, rows)
    scale = env[...]

    def store(n, value):
        hot[channel_rows(n)] = (value * scale).astype(BF16)

    rotate_back(wig, lambda k: rows[channel_rows(k)], store)
    total = dot_t(hot[...], one_hot(dst[...]).astype(BF16))
    updated[...] = (nodes[...].astype(F32) + total).astype(BF16)


def scatter_back(edge_in, wig, src, own_grad, low, high, rows, hot):
    load_transposed(edge_in, rows)

    def store(n, value):
        hot[channel_rows(n)] = value.astype(BF16)

    rotate_back(wig, lambda k: rows[channel_rows(k)], store)
    index = src[...]
    side = row_low()
    zero = jnp.zeros((LANES, LANES), F32)
    plain = one_hot(index, LANES)
    up = one_hot(index, LANES + 64)
    down = one_hot(index, 64)
    first = jnp.concatenate([jnp.where(side, plain, zero), jnp.where(side, zero, plain)], 0).astype(BF16)
    second = jnp.concatenate([jnp.where(side, zero, down), jnp.where(side, up, zero)], 0).astype(BF16)
    for n in range(0, TOP, 5):
        both = dot_t(hot[channel_rows(n, 5)], first)
        count = min(5, NODE - TOP - n)
        other = dot_t(hot[channel_rows(TOP + n, count)], second)
        if count < 5:
            other = jnp.concatenate([other, jnp.zeros(((5 - count) * 32, 256), F32)], 0)
        both = (both + other).astype(BF16)
        low[channel_rows(n, 5)] = both[:, :LANES]
        high[channel_rows(n, 5)] = both[:, LANES:]
    own_grad[...] = dot_t(hot[...], one_hot(index).astype(BF16))


def finish_backward(cot, own_grad, below, above, send, node_grad):
    match = one_hot(send[...])
    turned = pltpu.roll(match, 64, 1)
    side = lane_low()
    zero = jnp.zeros((LANES, LANES), F32)
    split = TOP * 32
    rest = (NODE - TOP) * 32
    top = dot_t(above[...], jnp.where(side, turned, zero).astype(BF16)) + dot_t(
        below[...], jnp.where(side, zero, turned).astype(BF16)
    )
    bottom = dot_t(above[:rest], jnp.where(side, zero, match).astype(BF16)) + dot_t(
        below[:rest], jnp.where(side, match, zero).astype(BF16)
    )
    node_grad[:split] = (cot[:split].astype(F32) + own_grad[:split] + top).astype(BF16)
    node_grad[split:] = (cot[split:].astype(F32) + own_grad[split:] + bottom).astype(BF16)


def call(body, outs, scratch=()):
    return pl.pallas_call(
        body,
        out_shape=[jax.ShapeDtypeStruct(shape, dtype) for shape, dtype in outs],
        scratch_shapes=[pltpu.VMEM(shape, dtype) for shape, dtype in scratch],
        compiler_params=pltpu.CompilerParams(vmem_limit_bytes=40 * 1024 * 1024),
    )


def shards(
    nodes,
    ghost_send,
    edge_src,
    edge_dst,
    wigner,
    envelope,
    w_zero,
    w_one_real,
    w_one_imag,
    w_two_real,
    w_two_imag,
    cotangent,
):
    weights = (w_zero, w_one_real, w_one_imag, w_two_real, w_two_imag)
    flat = NODE * 32
    node_rows = jnp.transpose(nodes, (1, 2, 0)).reshape(flat, LANES)
    cot_rows = jnp.transpose(cotangent, (1, 2, 0)).reshape(flat, LANES)
    wig = jnp.transpose(wigner, (2, 1, 0))
    send = ghost_send.reshape(1, LANES)
    src = edge_src.reshape(1, LANES)
    dst = edge_dst.reshape(1, LANES)
    env = envelope.reshape(1, LANES)
    count = lax.axis_size("space")
    onward = [(i, (i + 1) % count) for i in range(count)]
    backward = [(target, source) for source, target in onward]
    ghost = ((TOP * 32, LANES), BF16)
    packed = ((4, 32, WIDE), BF16)
    rows = ((WIDE, LANES), F32)

    def exchange(x):
        return lax.all_to_all(x, "morder", split_axis=0, concat_axis=0, tiled=True)

    low, high, edge_grad = call(prepare, [ghost, ghost, packed], [rows, ((flat, LANES), F32)])(
        node_rows, cot_rows, wig, send, dst, env
    )
    below = lax.ppermute(high, "space", onward)
    above = lax.ppermute(low, "space", backward)
    edge_grad = exchange(edge_grad)
    (grad_back,) = call(functools.partial(map_edges, False), [packed])(edge_grad, *weights)
    grad_back = exchange(grad_back)
    own_grad, low_grad, high_grad = call(
        scatter_back, [((flat, LANES), F32), ghost, ghost], [rows, ((flat, LANES), BF16)]
    )(grad_back, wig, src)
    below_grad = lax.ppermute(high_grad, "space", onward)
    above_grad = lax.ppermute(low_grad, "space", backward)
    (rotated,) = call(lower_rotate, [packed], [rows, ((flat, LANES), F32)])(
        node_rows, below, above, wig, src
    )
    rotated = exchange(rotated)
    (message,) = call(functools.partial(map_edges, True), [packed])(rotated, *weights)
    message = exchange(message)
    (updated,) = call(finish_forward, [((flat, LANES), BF16)], [rows, ((flat, LANES), BF16)])(
        node_rows, message, wig, env, dst
    )
    (node_grad,) = call(finish_backward, [((flat, LANES), BF16)])(
        cot_rows, own_grad, below_grad, above_grad, send
    )

    def restore(x):
        return jnp.transpose(x.reshape(NODE, 32, LANES), (2, 0, 1))

    return restore(updated), restore(node_grad)


def solution(mesh):
    in_specs = (
        P("space", None, "morder"),
        P("space"),
        P("space"),
        P("space"),
        P("space", None, None),
        P("space"),
        P(),
        P(),
        P(),
        P(),
        P(),
        P("space", None, "morder"),
    )
    out_specs = (P("space", None, "morder"), P("space", None, "morder"))
    return jax.shard_map(shards, mesh=mesh, in_specs=in_specs, out_specs=out_specs, check_vma=False)
```

profile of v0, /device:TPU:9, one launch (start us, length us, event | category | flops | bytes accessed | tf_op | source)
XLA Modules:
  0.0 94.7 jit_solution(10575661792640601575)
XLA Ops:
  0.6 0.0 copy-start.26
  0.6 0.0 copy-start.1
  0.7 1.0 %copy-done.1 = bf16[128,29,49]{0,1,2:T(8,128)(2,1)S(1)} copy-done((bf16[128,29,49]{0,1,2:T(8,128)(2,1)S(1)}, bf16[128,29,49]{0,1,2:T(8,128)(2,1)}, u32[]{:S(2)}) %copy-start.1) | copy-done | bytes 363800
  1.6 0.0 copy-start.6
  1.6 1.0 %copy-done.6 = bf16[128,49,32]{0,2,1:T(8,128)(2,1)S(1)} copy-done((bf16[128,49,32]{0,2,1:T(8,128)(2,1)S(1)}, bf16[128,49,32]{0,2,1:T(8,128)(2,1)}, u32[]{:S(2)}) %copy-start.6) | copy-done | bytes 401432
  2.6 1.0 %copy-done.13 = bf16[128,49,32]{0,2,1:T(8,128)(2,1)S(1)} copy-done((bf16[128,49,32]{0,2,1:T(8,128)(2,1)S(1)}, bf16[128,49,32]{0,2,1:T(8,128)(2,1)}, u32[]{:S(2)}) %copy-start.13) | copy-done | bytes 401432
  3.6 0.0 copy-start.20
  3.6 0.7 copy-done.20
  4.3 0.0 copy-start.22
  4.3 0.7 copy-done.22
  5.0 0.0 copy-start.24
  5.0 0.7 copy-done.24
  5.6 0.8 shard_map.131
  6.4 0.0 copy-start.19
  6.5 0.7 copy-done.19
  7.1 0.7 copy-done.27
  7.8 0.7 copy-done.28
  8.5 4.9 %all-to-all-start.2 = ((bf16[4,32,1024]{2,1,0:T(8,128)(2,1)}), bf16[4,32,1024]{2,1,0:T(8,128)(2,1)S(1)}, u32[]{:S(2)}, u32[]{:S(2)}) async-start(bf16[4,32,1024]{2,1,0:T(8,128)(2,1)} %copy-done.19), calls=%async_computation.2 | async-start | bytes 524288 | tf_op jit(solution)/shard_map/all_to_all | solution.py:297
  13.4 7.1 %collective-permute-start = (bf16[800,128]{1,0:T(8,128)(2,1)}, bf16[800,128]{1,0:T(8,128)(2,1)S(1)}, u32[]{:S(2)}, u32[]{:S(2)}) collective-permute-start(bf16[800,128]{1,0:T(8,128)(2,1)} %copy-done.28), channel_id=1, source_target_pairs={{0,4},{4,8},{8,12},{12,16},{16,20},{20,24},{24,28},{28,32},{32,36}... | collective-permute-start | bytes 614408 | tf_op jit(solution)/shard_map/ppermute | solution.py:302
  20.5 5.5 %collective-permute-start.1 = (bf16[800,128]{1,0:T(8,128)(2,1)}, bf16[800,128]{1,0:T(8,128)(2,1)S(1)}, u32[]{:S(2)}, u32[]{:S(2)}) collective-permute-start(bf16[800,128]{1,0:T(8,128)(2,1)} %copy-done.27), channel_id=1, source_target_pairs={{4,0},{8,4},{12,8},{16,12},{20,16},{24,20},{28,24},{32,28},{36,32}... | collective-permute-start | bytes 614408 | tf_op jit(solution)/shard_map/ppermute | solution.py:303
  26.0 0.5 collective-permute-done.below
  26.5 11.8 %collective-permute-done.1.above = bf16[800,128]{1,0:T(8,128)(2,1)S(1)} collective-permute-done((bf16[800,128]{1,0:T(8,128)(2,1)}, bf16[800,128]{1,0:T(8,128)(2,1)S(1)}, u32[]{:S(2)}, u32[]{:S(2)}) %collective-permute-start.1) | collective-permute-done | bytes 204832 | tf_op jit(solution)/shard_map/ppermute | solution.py:303
  38.2 0.0 copy-done.26
  38.2 0.0 copy-done.2
  38.3 1.0 %copy-done.7 = bf16[128,49,32]{0,2,1:T(8,128)(2,1)S(1)} copy-done((bf16[128,49,32]{0,2,1:T(8,128)(2,1)S(1)}, bf16[128,49,32]{0,2,1:T(8,128)(2,1)}, u32[]{:S(2)}) %copy-start.7) | copy-done | bytes 401432
  39.3 0.8 shard_map.132
  40.0 0.0 copy-start.16
  40.0 0.7 copy-done.16
  40.7 0.0 all-to-all-done.2.in_ref
  40.7 4.0 %all-to-all-start = ((bf16[4,32,1024]{2,1,0:T(8,128)(2,1)}), bf16[4,32,1024]{2,1,0:T(8,128)(2,1)}, u32[]{:S(2)}, u32[]{:S(2)}) async-start(bf16[4,32,1024]{2,1,0:T(8,128)(2,1)} %copy-done.16), calls=%async_computation | async-start | bytes 524288 | tf_op jit(solution)/shard_map/all_to_all | solution.py:297
  44.8 0.0 copy-done.3
  44.8 0.0 copy-done
  44.8 0.0 copy-start.4
  44.8 1.3 %copy-done.4 = bf16[768,768]{1,0:T(8,128)(2,1)S(1)} copy-done((bf16[768,768]{1,0:T(8,128)(2,1)S(1)}, bf16[768,768]{1,0:T(8,128)(2,1)}, u32[]{:S(2)}) %copy-start.4) | copy-done | bytes 1179672
  46.1 1.1 %copy-done.9 = bf16[640,640]{1,0:T(8,128)(2,1)S(1)} copy-done((bf16[640,640]{1,0:T(8,128)(2,1)S(1)}, bf16[640,640]{1,0:T(8,128)(2,1)}, u32[]{:S(2)}) %copy-start.9) | copy-done | bytes 819224
  47.2 1.1 %copy-done.11 = bf16[640,640]{1,0:T(8,128)(2,1)S(1)} copy-done((bf16[640,640]{1,0:T(8,128)(2,1)S(1)}, bf16[640,640]{1,0:T(8,128)(2,1)}, u32[]{:S(2)}) %copy-start.11) | copy-done | bytes 819224
  48.4 1.9 %shard_map.135 = bf16[4,32,1024]{2,1,0:T(8,128)(2,1)S(1)} custom-call(bf16[4,32,1024]{2,1,0:T(8,128)(2,1)S(1)} %all-to-all-done.2.in_ref, bf16[896,896]{1,0:T(8,128)(2,1)S(1)} %copy-done, bf16[768,768]{1,0:T(8,128)(2,1)S(1)} %copy-done.3, bf16[768,768]{1,0:T(8,128)(2,1)S(1)} %copy-done.4, bf16[640,640]{1,0:T(8,128)(2,1)S(1)} %copy-done.9, ...), custom_call_target="tpu_custom_call" | custom-call | tf_op jit(solution)/shard_map/pallas_call | solution.py:305
  50.2 0.0 copy-start.15
  50.3 0.7 copy-done.15
  50.9 0.0 all-to-all-done.in_ref
  51.0 4.0 %all-to-all-start.3 = ((bf16[4,32,1024]{2,1,0:T(8,128)(2,1)}), bf16[4,32,1024]{2,1,0:T(8,128)(2,1)}, u32[]{:S(2)}, u32[]{:S(2)}) async-start(bf16[4,32,1024]{2,1,0:T(8,128)(2,1)} %copy-done.15), calls=%async_computation.3 | async-start | bytes 524288 | tf_op jit(solution)/shard_map/all_to_all | solution.py:297
  55.0 0.0 copy-start.5
  55.0 1.3 %copy-done.5 = bf16[768,768]{1,0:T(8,128)(2,1)S(1)} copy-done((bf16[768,768]{1,0:T(8,128)(2,1)S(1)}, bf16[768,768]{1,0:T(8,128)(2,1)}, u32[]{:S(2)}) %copy-start.5) | copy-done | bytes 1179672
  56.3 1.1 %copy-done.10 = bf16[640,640]{1,0:T(8,128)(2,1)S(1)} copy-done((bf16[640,640]{1,0:T(8,128)(2,1)S(1)}, bf16[640,640]{1,0:T(8,128)(2,1)}, u32[]{:S(2)}) %copy-start.10) | copy-done | bytes 819224
  57.4 1.1 %copy-done.12 = bf16[640,640]{1,0:T(8,128)(2,1)S(1)} copy-done((bf16[640,640]{1,0:T(8,128)(2,1)S(1)}, bf16[640,640]{1,0:T(8,128)(2,1)}, u32[]{:S(2)}) %copy-start.12) | copy-done | bytes 819224
  58.6 3.0 %shard_map.133 = bf16[4,32,1024]{2,1,0:T(8,128)(2,1)} custom-call(bf16[4,32,1024]{2,1,0:T(8,128)(2,1)} %all-to-all-done.in_ref, bf16[896,896]{1,0:T(8,128)(2,1)S(1)} %copy-done, bf16[768,768]{1,0:T(8,128)(2,1)S(1)} %copy-done.3, bf16[768,768]{1,0:T(8,128)(2,1)S(1)} %copy-done.5, bf16[640,640]{1,0:T(8,128)(2,1)S(1)} %copy-done.10, bf16[640,640]{1,0:T(8,128)(2,1)S(1)} %copy-done.12), custom_call_target="tpu_custom_call" | custom-call | tf_op jit(solution)/shard_map/pallas_call | solution.py:316
  61.5 0.0 all-to-all-done.3.edge_in
  61.6 4.6 %all-to-all-start.1 = ((bf16[4,32,1024]{2,1,0:T(8,128)(2,1)}), bf16[4,32,1024]{2,1,0:T(8,128)(2,1)S(1)}, u32[]{:S(2)}, u32[]{:S(2)}) async-start(bf16[4,32,1024]{2,1,0:T(8,128)(2,1)} %shard_map.133), calls=%async_computation.1 | async-start | bytes 524288 | tf_op jit(solution)/shard_map/all_to_all | solution.py:297
  66.1 1.7 %shard_map.136 = (f32[1568,128]{1,0:T(8,128)S(1)}, bf16[800,128]{1,0:T(8,128)(2,1)S(1)}, bf16[800,128]{1,0:T(8,128)(2,1)S(1)}) custom-call(bf16[4,32,1024]{2,1,0:T(8,128)(2,1)} %all-to-all-done.3.edge_in, bf16[49,29,128]{2,1,0:T(8,128)(2,1)S(1)} %bitcast.19, s32[1,128]{1,0:T(1,128)S(1)} %bitcast.33), custom_call_target="tpu_custom_call" | custom-call | tf_op jit(solution)/shard_map/pallas_call | solution.py:307
  67.9 0.0 copy-start.17
  67.9 0.9 copy-done.17
  68.8 7.2 %collective-permute-start.2 = (bf16[800,128]{1,0:T(8,128)(2,1)S(1)}, bf16[800,128]{1,0:T(8,128)(2,1)S(1)}, u32[]{:S(2)}, u32[]{:S(2)}) collective-permute-start(bf16[800,128]{1,0:T(8,128)(2,1)S(1)} %get-tuple-element.12), channel_id=1, source_target_pairs={{0,4},{4,8},{8,12},{12,16},{16,20},{20,24},{24,28},{28,32},{32,36}... | collective-permute-start | bytes 614408 | tf_op jit(solution)/shard_map/ppermute | solution.py:310
  76.0 1.9 %collective-permute-start.3 = (bf16[800,128]{1,0:T(8,128)(2,1)S(1)}, bf16[800,128]{1,0:T(8,128)(2,1)S(1)}, u32[]{:S(2)}, u32[]{:S(2)}) collective-permute-start(bf16[800,128]{1,0:T(8,128)(2,1)S(1)} %get-tuple-element.13), channel_id=1, source_target_pairs={{4,0},{8,4},{12,8},{16,12},{20,16},{24,20},{28,24},{32,28},{36,32}... | collective-permute-start | bytes 614408 | tf_op jit(solution)/shard_map/ppermute | solution.py:311
  77.9 0.0 all-to-all-done.1.edge_in
  77.9 0.0 copy-done.8
  77.9 0.0 copy-done.21
  77.9 0.0 copy-done.23
  77.9 1.4 %shard_map.134 = bf16[1568,128]{1,0:T(8,128)(2,1)} custom-call(bf16[1568,128]{1,0:T(8,128)(2,1)S(1)} %bitcast.23, bf16[4,32,1024]{2,1,0:T(8,128)(2,1)S(1)} %all-to-all-done.1.edge_in, bf16[49,29,128]{2,1,0:T(8,128)(2,1)S(1)} %bitcast.20, f32[1,128]{1,0:T(1,128)S(1)} %bitcast.29, s32[1,128]{1,0:T(1,128)S(1)} %bitcast.27), custom_call_target="tpu_custom_call" | custom-call | tf_op jit(solution)/shard_map/pallas_call | solution.py:318
  79.3 5.9 %collective-permute-done.2.below = bf16[800,128]{1,0:T(8,128)(2,1)S(1)} collective-permute-done((bf16[800,128]{1,0:T(8,128)(2,1)S(1)}, bf16[800,128]{1,0:T(8,128)(2,1)S(1)}, u32[]{:S(2)}, u32[]{:S(2)}) %collective-permute-start.2) | collective-permute-done | bytes 204832 | tf_op jit(solution)/shard_map/ppermute | solution.py:310
  85.2 8.3 %collective-permute-done.3.above = bf16[800,128]{1,0:T(8,128)(2,1)S(1)} collective-permute-done((bf16[800,128]{1,0:T(8,128)(2,1)S(1)}, bf16[800,128]{1,0:T(8,128)(2,1)S(1)}, u32[]{:S(2)}, u32[]{:S(2)}) %collective-permute-start.3) | collective-permute-done | bytes 204832 | tf_op jit(solution)/shard_map/ppermute | solution.py:311
  93.5 0.0 copy-done.14
  93.5 0.0 copy-done.25
  93.5 0.0 copy-done.18
  93.5 1.2 %shard_map.137 = bf16[1568,128]{1,0:T(8,128)(2,1)} custom-call(bf16[1568,128]{1,0:T(8,128)(2,1)S(1)} %bitcast.25, f32[1568,128]{1,0:T(8,128)S(1)} %copy-done.18, bf16[800,128]{1,0:T(8,128)(2,1)S(1)} %collective-permute-done.2.below, bf16[800,128]{1,0:T(8,128)(2,1)S(1)} %collective-permute-done.3.above, s32[1,128]{1,0:T(1,128)S(1)} %bitcast.31), custom_call_target="tpu_custom_call" | custom-call | tf_op jit(solution)/shard_map/pallas_call | solution.py:321
  (17 shorter events, 0.0 us)
Async XLA Ops:
  0.6 37.6 %copy-start.26 = (s32[128]{0:T(128)S(1)}, s32[128]{0:T(128)}, u32[]{:S(2)}) copy-start(s32[128]{0:T(128)} %param.14) | copy-start | bytes 1540
  0.6 1.0 %copy-start.1 = (bf16[128,29,49]{0,1,2:T(8,128)(2,1)S(1)}, bf16[128,29,49]{0,1,2:T(8,128)(2,1)}, u32[]{:S(2)}) copy-start(bf16[128,29,49]{0,1,2:T(8,128)(2,1)} %param.16) | copy-start | bytes 1091332
  1.6 1.0 %copy-start.6 = (bf16[128,49,32]{0,2,1:T(8,128)(2,1)S(1)}, bf16[128,49,32]{0,2,1:T(8,128)(2,1)}, u32[]{:S(2)}) copy-start(bf16[128,49,32]{0,2,1:T(8,128)(2,1)} %param.12) | copy-start | bytes 1204228
  2.6 1.0 %copy-start.13 = (bf16[128,49,32]{0,2,1:T(8,128)(2,1)S(1)}, bf16[128,49,32]{0,2,1:T(8,128)(2,1)}, u32[]{:S(2)}) copy-start(bf16[128,49,32]{0,2,1:T(8,128)(2,1)} %param.23) | copy-start | bytes 1204228
  3.6 0.7 copy-start.20
  4.3 0.7 copy-start.22
  5.0 0.7 copy-start.24
  5.6 32.6 %copy-start.2 = (bf16[128,29,49]{0,1,2:T(8,128)(2,1)S(1)}, bf16[128,29,49]{0,1,2:T(8,128)(2,1)}, u32[]{:S(2)}) copy-start(bf16[128,29,49]{0,1,2:T(8,128)(2,1)} %param.16) | copy-start | bytes 1091332
  5.6 39.2 %copy-start.3 = (bf16[768,768]{1,0:T(8,128)(2,1)S(1)}, bf16[768,768]{1,0:T(8,128)(2,1)}, u32[]{:S(2)}) copy-start(bf16[768,768]{1,0:T(8,128)(2,1)} %w_one_real.3) | copy-start | bytes 3538948
  6.4 0.7 copy-start.19
  7.1 0.7 copy-start.27
  7.8 0.7 copy-start.28
  8.5 36.3 %copy-start = (bf16[896,896]{1,0:T(8,128)(2,1)S(1)}, bf16[896,896]{1,0:T(8,128)(2,1)}, u32[]{:S(2)}) copy-start(bf16[896,896]{1,0:T(8,128)(2,1)} %w_zero.3) | copy-start | bytes 4816900
  8.5 32.2 %all-to-all-start.2 = ((bf16[4,32,1024]{2,1,0:T(8,128)(2,1)}), bf16[4,32,1024]{2,1,0:T(8,128)(2,1)S(1)}, u32[]{:S(2)}, u32[]{:S(2)}) async-start(bf16[4,32,1024]{2,1,0:T(8,128)(2,1)} %copy-done.19), calls=%async_computation.2 | async-start | bytes 524288 | tf_op jit(solution)/shard_map/all_to_all | solution.py:297
  13.4 13.1 %collective-permute-start = (bf16[800,128]{1,0:T(8,128)(2,1)}, bf16[800,128]{1,0:T(8,128)(2,1)S(1)}, u32[]{:S(2)}, u32[]{:S(2)}) collective-permute-start(bf16[800,128]{1,0:T(8,128)(2,1)} %copy-done.28), channel_id=1, source_target_pairs={{0,4},{4,8},{8,12},{12,16},{16,20},{20,24},{24,28},{28,32},{32,36}... | collective-permute-start | bytes 614408 | tf_op jit(solution)/shard_map/ppermute | solution.py:302
  20.5 17.8 %collective-permute-start.1 = (bf16[800,128]{1,0:T(8,128)(2,1)}, bf16[800,128]{1,0:T(8,128)(2,1)S(1)}, u32[]{:S(2)}, u32[]{:S(2)}) collective-permute-start(bf16[800,128]{1,0:T(8,128)(2,1)} %copy-done.27), channel_id=1, source_target_pairs={{4,0},{8,4},{12,8},{16,12},{20,16},{24,20},{28,24},{32,28},{36,32}... | collective-permute-start | bytes 614408 | tf_op jit(solution)/shard_map/ppermute | solution.py:303
  38.3 1.0 %copy-start.7 = (bf16[128,49,32]{0,2,1:T(8,128)(2,1)S(1)}, bf16[128,49,32]{0,2,1:T(8,128)(2,1)}, u32[]{:S(2)}) copy-start(bf16[128,49,32]{0,2,1:T(8,128)(2,1)} %param.12) | copy-start | bytes 1204228
  40.0 0.7 copy-start.16
  40.7 10.2 %all-to-all-start = ((bf16[4,32,1024]{2,1,0:T(8,128)(2,1)}), bf16[4,32,1024]{2,1,0:T(8,128)(2,1)}, u32[]{:S(2)}, u32[]{:S(2)}) async-start(bf16[4,32,1024]{2,1,0:T(8,128)(2,1)} %copy-done.16), calls=%async_computation | async-start | bytes 524288 | tf_op jit(solution)/shard_map/all_to_all | solution.py:297
  44.8 1.3 %copy-start.4 = (bf16[768,768]{1,0:T(8,128)(2,1)S(1)}, bf16[768,768]{1,0:T(8,128)(2,1)}, u32[]{:S(2)}) copy-start(bf16[768,768]{1,0:T(8,128)(2,1)} %w_one_imag.3) | copy-start | bytes 3538948
  46.1 1.1 %copy-start.9 = (bf16[640,640]{1,0:T(8,128)(2,1)S(1)}, bf16[640,640]{1,0:T(8,128)(2,1)}, u32[]{:S(2)}) copy-start(bf16[640,640]{1,0:T(8,128)(2,1)} %w_two_real.3) | copy-start | bytes 2457604
  47.2 1.1 %copy-start.11 = (bf16[640,640]{1,0:T(8,128)(2,1)S(1)}, bf16[640,640]{1,0:T(8,128)(2,1)}, u32[]{:S(2)}) copy-start(bf16[640,640]{1,0:T(8,128)(2,1)} %w_two_imag.3) | copy-start | bytes 2457604
  50.2 0.7 copy-start.15
  51.0 10.6 %all-to-all-start.3 = ((bf16[4,32,1024]{2,1,0:T(8,128)(2,1)}), bf16[4,32,1024]{2,1,0:T(8,128)(2,1)}, u32[]{:S(2)}, u32[]{:S(2)}) async-start(bf16[4,32,1024]{2,1,0:T(8,128)(2,1)} %copy-done.15), calls=%async_computation.3 | async-start | bytes 524288 | tf_op jit(solution)/shard_map/all_to_all | solution.py:297
  55.0 1.3 %copy-start.5 = (bf16[768,768]{1,0:T(8,128)(2,1)S(1)}, bf16[768,768]{1,0:T(8,128)(2,1)}, u32[]{:S(2)}) copy-start(bf16[768,768]{1,0:T(8,128)(2,1)} %w_one_imag.3) | copy-start | bytes 3538948
  56.3 1.1 %copy-start.10 = (bf16[640,640]{1,0:T(8,128)(2,1)S(1)}, bf16[640,640]{1,0:T(8,128)(2,1)}, u32[]{:S(2)}) copy-start(bf16[640,640]{1,0:T(8,128)(2,1)} %w_two_real.3) | copy-start | bytes 2457604
  57.4 1.1 %copy-start.12 = (bf16[640,640]{1,0:T(8,128)(2,1)S(1)}, bf16[640,640]{1,0:T(8,128)(2,1)}, u32[]{:S(2)}) copy-start(bf16[640,640]{1,0:T(8,128)(2,1)} %w_two_imag.3) | copy-start | bytes 2457604
  61.5 16.4 %copy-start.8 = (bf16[128,49,32]{0,2,1:T(8,128)(2,1)S(1)}, bf16[128,49,32]{0,2,1:T(8,128)(2,1)}, u32[]{:S(2)}) copy-start(bf16[128,49,32]{0,2,1:T(8,128)(2,1)} %param.12) | copy-start | bytes 1204228
  61.5 16.4 %copy-start.21 = (s32[128]{0:T(128)S(1)}, s32[128]{0:T(128)}, u32[]{:S(2)}) copy-start(s32[128]{0:T(128)} %param.15) | copy-start | bytes 1540
  61.5 16.4 %copy-start.23 = (f32[128]{0:T(128)S(1)}, f32[128]{0:T(128)}, u32[]{:S(2)}) copy-start(f32[128]{0:T(128)} %param.17) | copy-start | bytes 1540
  61.6 16.3 %all-to-all-start.1 = ((bf16[4,32,1024]{2,1,0:T(8,128)(2,1)}), bf16[4,32,1024]{2,1,0:T(8,128)(2,1)S(1)}, u32[]{:S(2)}, u32[]{:S(2)}) async-start(bf16[4,32,1024]{2,1,0:T(8,128)(2,1)} %shard_map.133), calls=%async_computation.1 | async-start | bytes 524288 | tf_op jit(solution)/shard_map/all_to_all | solution.py:297
  66.1 27.4 %copy-start.14 = (bf16[128,49,32]{0,2,1:T(8,128)(2,1)S(1)}, bf16[128,49,32]{0,2,1:T(8,128)(2,1)}, u32[]{:S(2)}) copy-start(bf16[128,49,32]{0,2,1:T(8,128)(2,1)} %param.23) | copy-start | bytes 1204228
  66.1 27.4 %copy-start.25 = (s32[128]{0:T(128)S(1)}, s32[128]{0:T(128)}, u32[]{:S(2)}) copy-start(s32[128]{0:T(128)} %param.13) | copy-start | bytes 1540
  67.9 0.9 copy-start.17
  68.8 24.7 %copy-start.18 = (f32[1568,128]{1,0:T(8,128)S(1)}, f32[1568,128]{1,0:T(8,128)}, u32[]{:S(2)}) copy-start(f32[1568,128]{1,0:T(8,128)} %copy-done.17) | copy-start | bytes 2408452
  68.8 16.4 %collective-permute-start.2 = (bf16[800,128]{1,0:T(8,128)(2,1)S(1)}, bf16[800,128]{1,0:T(8,128)(2,1)S(1)}, u32[]{:S(2)}, u32[]{:S(2)}) collective-permute-start(bf16[800,128]{1,0:T(8,128)(2,1)S(1)} %get-tuple-element.12), channel_id=1, source_target_pairs={{0,4},{4,8},{8,12},{12,16},{16,20},{20,24},{24,28},{28,32},{32,36}... | collective-permute-start | bytes 614408 | tf_op jit(solution)/shard_map/ppermute | solution.py:310
  76.0 17.6 %collective-permute-start.3 = (bf16[800,128]{1,0:T(8,128)(2,1)S(1)}, bf16[800,128]{1,0:T(8,128)(2,1)S(1)}, u32[]{:S(2)}, u32[]{:S(2)}) collective-permute-start(bf16[800,128]{1,0:T(8,128)(2,1)S(1)} %get-tuple-element.13), channel_id=1, source_target_pairs={{4,0},{8,4},{12,8},{16,12},{20,16},{24,20},{28,24},{32,28},{36,32}... | collective-permute-start | bytes 614408 | tf_op jit(solution)/shard_map/ppermute | solution.py:311
where the time goes:
time: 95.8 us; the launch traced here: 94.7 us
  starting transfers between devices  39.2 us (41%)
  waiting for transfers between devices  26.5 us (28%)
  local copies, waits for them, and re-layouts  17.4 us (18%)
  Pallas kernels  10.8 us (11%)
    all_to_all x4, starting transfers between devices, exchange(): return lax.all_to_all(x, 'morder', split_axis=0, concat_axis=0, tiled=True)  17.5 us
    unnamed x58, local copies, waits for them, and re-layouts  17.4 us
    ppermute x1, waiting for transfers between devices, shards(): above = lax.ppermute(low, 'space', backward)  11.8 us
    ppermute x1, waiting for transfers between devices, shards(): above_grad = lax.ppermute(low_grad, 'space', backward)  8.31 us
    ppermute x1, starting transfers between devices, shards(): below_grad = lax.ppermute(high_grad, 'space', onward)  7.16 us
    ppermute x1, starting transfers between devices, shards(): below = lax.ppermute(high, 'space', onward)  7.07 us
    ppermute x1, waiting for transfers between devices, shards(): below_grad = lax.ppermute(high_grad, 'space', onward)  5.91 us
    ppermute x1, starting transfers between devices, shards(): above = lax.ppermute(low, 'space', backward)  5.51 us
  transfers between devices with their start and end apart: 8, of which 4 were waited for; matrix products, arithmetic and copies ran while one was open for 0% of the time, Pallas kernels for 9%

commit v1 on v0

v1 whole, which is shorter than its diff:
```python
import jax
import jax.numpy as jnp
from jax import lax
from jax.experimental import pallas as pl
from jax.experimental.pallas import tpu as pltpu
from jax.sharding import PartitionSpec as P

F32, BF16 = jnp.float32, jnp.bfloat16
LANES = 128
TOP = 25
NODE = 49
EDGE = 29
WIDE = 1024
PARTS = ((0, 7), (7, 6), (13, 6), (19, 5), (24, 5))


def degree_rows(degree):
    rows = [degree]
    if degree >= 1:
        rows += [6 + degree, 12 + degree]
    if degree >= 2:
        rows += [17 + degree, 22 + degree]
    return rows


def dot(a, b):
    return jnp.dot(a, b, preferred_element_type=F32)


def dot_t(a, b):
    return lax.dot_general(a, b, (((1,), (1,)), ((), ())), preferred_element_type=F32)


def one_hot(index_row, offset=0):
    rows = lax.broadcasted_iota(jnp.int32, (LANES, LANES), 0) + offset
    return jnp.where(rows == index_row, 1.0, 0.0).astype(F32)


def lane_low():
    return lax.broadcasted_iota(jnp.int32, (LANES, LANES), 1) < LANES // 2


def row_low():
    return lax.broadcasted_iota(jnp.int32, (LANES, LANES), 0) < LANES // 2


def rotate(rot_ref, load, store):
    for degree in range(7):
        columns = range(degree * degree, (degree + 1) * (degree + 1))
        for k in degree_rows(degree):
            total = None
            for n in columns:
                term = rot_ref[n, k : k + 1, :].astype(F32) * load(n)
                total = term if total is None else total + term
            store(k, total)


def rotate_back(rot_ref, load, store):
    for degree in range(7):
        for n in range(degree * degree, (degree + 1) * (degree + 1)):
            total = None
            for k in degree_rows(degree):
                term = rot_ref[n, k : k + 1, :].astype(F32) * load(k)
                total = term if total is None else total + term
            store(n, total)


def channel_rows(n, count=1):
    return slice(n * 32, (n + count) * 32)


def swap_blocks(blocks):
    group = lax.broadcasted_iota(jnp.int32, blocks[0].shape, 1) // 32
    low = group < 2
    a0 = jnp.where(low, blocks[0], pltpu.roll(blocks[2], 64, 1))
    a2 = jnp.where(low, pltpu.roll(blocks[0], 64, 1), blocks[2])
    a1 = jnp.where(low, blocks[1], pltpu.roll(blocks[3], 64, 1))
    a3 = jnp.where(low, pltpu.roll(blocks[1], 64, 1), blocks[3])
    even = (group % 2) == 0
    b0 = jnp.where(even, a0, pltpu.roll(a1, 32, 1))
    b1 = jnp.where(even, pltpu.roll(a0, 96, 1), a1)
    b2 = jnp.where(even, a2, pltpu.roll(a3, 32, 1))
    b3 = jnp.where(even, pltpu.roll(a2, 96, 1), a3)
    return [b0, b1, b2, b3]


CHUNKS = ((0, 2), (2, 5), (5, 8))


def store_transposed(rows_ref, out_ref, first, last):
    for group in range(first, last):
        piece = rows_ref[group * LANES : (group + 1) * LANES, :].T.astype(BF16)
        for part in range(4):
            out_ref[part, group] = piece[part * 32 : (part + 1) * 32]


def load_transposed(in_ref, rows_ref, first, last):
    for group in range(first, last):
        piece = jnp.concatenate([in_ref[part, group].astype(F32) for part in range(4)], axis=0)
        rows_ref[group * LANES : (group + 1) * LANES, :] = piece.T


class Exchange:
    def __init__(self, send, recv, send_sem, recv_sem, base):
        self.send, self.recv = send, recv
        self.space, self.me = lax.axis_index("space"), lax.axis_index("morder")
        self.copies = {}
        for piece, (first, last) in enumerate(CHUNKS):
            for step in (1, 2, 3):
                target = lax.rem(self.me + step, 4)
                slot = base + piece * 3 + step - 1
                span = pl.ds(first, last - first)
                self.copies[piece, step] = pltpu.make_async_remote_copy(
                    src_ref=send.at[target, span],
                    dst_ref=recv.at[self.me, span],
                    send_sem=send_sem.at[slot],
                    recv_sem=recv_sem.at[slot],
                    device_id=(self.space, target),
                    device_id_type=pl.DeviceIdType.MESH,
                )

    def start(self, piece):
        for step in (2, 1, 3):
            self.copies[piece, step].start()
        first, last = CHUNKS[piece]
        self.recv[self.me, first:last] = self.send[self.me, first:last]

    def arrived(self, piece):
        for step in (1, 2, 3):
            self.copies[piece, step].wait_recv()

    def sent(self):
        for copy in self.copies.values():
            copy.wait_send()


def gather_group(in_ref, group):
    return swap_blocks([in_ref[i, group].astype(F32) for i in range(4)])


def map_edges(forward, before, after, weights):
    w_zero, w_one_real, w_one_imag, w_two_real, w_two_imag = weights
    product = dot if forward else dot_t
    blocks, results = [], []

    def take(piece):
        before.arrived(piece)
        for group in range(*CHUNKS[piece]):
            blocks.extend(gather_group(before.recv, group))

    def part(i):
        start, count = PARTS[i]
        return jnp.concatenate(blocks[start : start + count], 1).astype(BF16)

    def put(value):
        results.extend(value[:, i * LANES : (i + 1) * LANES] for i in range(value.shape[1] // LANES))

    def pair(first, real, imag):
        both = jnp.concatenate([part(first), part(first + 1)], 0)
        straight = product(both, real[...])
        crossed = product(both, imag[...])
        if forward:
            put(straight[:32] - crossed[32:])
            put(straight[32:] + crossed[:32])
        else:
            put(straight[:32] + crossed[32:])
            put(straight[32:] - crossed[:32])

    def give(piece):
        for group in range(*CHUNKS[piece]):
            for i, value in enumerate(swap_blocks(results[4 * group : 4 * group + 4])):
                after.send[i, group] = value.astype(BF16)
        after.start(piece)

    take(0)
    put(product(part(0), w_zero[...]))
    take(1)
    pair(1, w_one_real, w_one_imag)
    give(0)
    take(2)
    pair(3, w_two_real, w_two_imag)
    give(1)
    results.extend([jnp.zeros_like(results[0])] * 3)
    give(2)


def ghost_pack(product, source, first, second, low, high):
    for n in range(0, TOP, 5):
        both = product(source[channel_rows(n, 5)], first)
        count = min(5, NODE - TOP - n)
        other = product(source[channel_rows(TOP + n, count)], second)
        if count < 5:
            other = jnp.concatenate([other, jnp.zeros(((5 - count) * 32, 256), F32)], 0)
        both = (both + other).astype(BF16)
        low[channel_rows(n, 5)] = both[:, :LANES]
        high[channel_rows(n, 5)] = both[:, LANES:]


def layer(
    nodes_hbm,
    cot_hbm,
    wig_hbm,
    send_ref,
    src_ref,
    dst_ref,
    env_ref,
    w0_hbm,
    w1r_hbm,
    w1i_hbm,
    w2r_hbm,
    w2i_hbm,
    updated_hbm,
    node_grad_hbm,
    nodes,
    cot,
    wig,
    w0,
    w1r,
    w1i,
    w2r,
    w2i,
    low,
    high,
    below,
    above,
    low_grad,
    high_grad,
    below_grad,
    above_grad,
    edge_send,
    edge_recv,
    back_send,
    back_recv,
    rot_send,
    rot_recv,
    msg_send,
    msg_recv,
    rows,
    hot,
    hot_half,
    own_grad,
    updated,
    node_grad,
    local_sem,
    out_sem,
    send_sem,
    recv_sem,
    ghost_send_sem,
    ghost_recv_sem,
):
    space, me = lax.axis_index("space"), lax.axis_index("morder")
    domains = lax.axis_size("space")
    upper = lax.rem(space + 1, domains)
    lower = lax.rem(space + domains - 1, domains)
    peers = [(upper, me), (lower, me)] + [(space, lax.rem(me + step, 4)) for step in (1, 2, 3)]
    barrier = pltpu.get_barrier_semaphore()
    for peer in peers:
        pl.semaphore_signal(barrier, inc=1, device_id=peer, device_id_type=pl.DeviceIdType.MESH)
    loads = [
        pltpu.make_async_copy(a, b, local_sem.at[i])
        for i, (a, b) in enumerate(
            (
                (cot_hbm, cot),
                (wig_hbm, wig),
                (nodes_hbm, nodes),
                (w0_hbm, w0),
                (w1r_hbm, w1r),
                (w1i_hbm, w1i),
                (w2r_hbm, w2r),
                (w2i_hbm, w2i),
            )
        )
    ]
    for load in loads:
        load.start()
    weights = (w0, w1r, w1i, w2r, w2i)

    def ghost_copy(slot, source, target, device):
        return pltpu.make_async_remote_copy(
            src_ref=source,
            dst_ref=target,
            send_sem=ghost_send_sem.at[slot],
            recv_sem=ghost_recv_sem.at[slot],
            device_id=(device, me),
            device_id_type=pl.DeviceIdType.MESH,
        )

    ghosts = [
        ghost_copy(0, high, below, upper),
        ghost_copy(1, low, above, lower),
        ghost_copy(2, high_grad, below_grad, upper),
        ghost_copy(3, low_grad, above_grad, lower),
    ]
    pieces = len(CHUNKS) * 3
    edge_x = Exchange(edge_send, edge_recv, send_sem, recv_sem, 0)
    back_x = Exchange(back_send, back_recv, send_sem, recv_sem, pieces)
    rot_x = Exchange(rot_send, rot_recv, send_sem, recv_sem, 2 * pieces)
    msg_x = Exchange(msg_send, msg_recv, send_sem, recv_sem, 3 * pieces)

    side, rside = lane_low(), row_low()
    zero = jnp.zeros((LANES, LANES), F32)
    scale = env_ref[...]
    rows[EDGE * 32 :] = jnp.zeros((WIDE - EDGE * 32, LANES), F32)
    split = TOP * 32
    rest = (NODE - TOP) * 32

    loads[0].wait()
    hot[...] = dot(cot[...], one_hot(dst_ref[...]).astype(BF16))
    loads[1].wait()

    def store_scaled(k, value):
        rows[channel_rows(k)] = value * scale

    def store_plain(k, value):
        rows[channel_rows(k)] = value

    rotate(wig, lambda n: hot[channel_rows(n)], store_scaled)
    for piece, (first, last) in enumerate(CHUNKS):
        store_transposed(rows, edge_send, first, last)
        if piece == 0:
            pl.semaphore_wait(barrier, len(peers))
        edge_x.start(piece)

    match = one_hot(send_ref[...])
    turned = pltpu.roll(match, 64, 1)
    loads[2].wait()
    ghost_pack(
        dot,
        nodes,
        jnp.concatenate([jnp.where(side, match, zero), jnp.where(side, zero, match)], 1).astype(BF16),
        jnp.concatenate([jnp.where(side, zero, turned), jnp.where(side, turned, zero)], 1).astype(BF16),
        low,
        high,
    )
    ghosts[0].start()
    ghosts[1].start()
    index = src_ref[...]
    own = one_hot(index).astype(BF16)
    plain = one_hot(index, LANES)
    up = one_hot(index, LANES + 64)
    down = one_hot(index, 64)
    hot[...] = dot(nodes[...], own)

    for load in loads[3:]:
        load.wait()
    map_edges(False, edge_x, back_x, weights)

    ghosts[0].wait_recv()
    ghosts[1].wait_recv()
    hot[:split] += dot(below[...], jnp.where(rside, zero, down).astype(BF16)) + dot(
        above[...], jnp.where(rside, up, zero).astype(BF16)
    )
    hot[split:] += dot(below[:rest], jnp.where(rside, plain, zero).astype(BF16)) + dot(
        above[:rest], jnp.where(rside, zero, plain).astype(BF16)
    )
    rotate(wig, lambda n: hot[channel_rows(n)], store_plain)
    for piece, (first, last) in enumerate(CHUNKS):
        store_transposed(rows, rot_send, first, last)
        rot_x.start(piece)

    for piece, (first, last) in enumerate(CHUNKS):
        back_x.arrived(piece)
        load_transposed(back_recv, rows, first, last)

    def store_half(n, value):
        hot_half[channel_rows(n)] = value.astype(BF16)

    rotate_back(wig, lambda k: rows[channel_rows(k)], store_half)
    ghost_pack(
        dot_t,
        hot_half,
        jnp.concatenate([jnp.where(rside, plain, zero), jnp.where(rside, zero, plain)], 0).astype(BF16),
        jnp.concatenate([jnp.where(rside, zero, down), jnp.where(rside, up, zero)], 0).astype(BF16),
        low_grad,
        high_grad,
    )
    ghosts[2].start()
    ghosts[3].start()
    own_grad[...] = dot_t(hot_half[...], own) + cot[...].astype(F32)

    map_edges(True, rot_x, msg_x, weights)

    for piece, (first, last) in enumerate(CHUNKS):
        msg_x.arrived(piece)
        load_transposed(msg_recv, rows, first, last)

    def store_message(n, value):
        hot_half[channel_rows(n)] = (value * scale).astype(BF16)

    rotate_back(wig, lambda k: rows[channel_rows(k)], store_message)
    total = dot_t(hot_half[...], one_hot(dst_ref[...]).astype(BF16))
    updated[...] = (nodes[...].astype(F32) + total).astype(BF16)
    write = pltpu.make_async_copy(updated, updated_hbm, out_sem.at[0])
    write.start()

    ghosts[2].wait_recv()
    ghosts[3].wait_recv()
    match = one_hot(send_ref[...])
    turned = pltpu.roll(match, 64, 1)
    top = dot_t(above_grad[...], jnp.where(side, turned, zero).astype(BF16)) + dot_t(
        below_grad[...], jnp.where(side, zero, turned).astype(BF16)
    )
    node_grad[:split] = (own_grad[:split] + top).astype(BF16)
    bottom = dot_t(above_grad[:rest], jnp.where(side, zero, match).astype(BF16)) + dot_t(
        below_grad[:rest], jnp.where(side, match, zero).astype(BF16)
    )
    node_grad[split:] = (own_grad[split:] + bottom).astype(BF16)
    last_write = pltpu.make_async_copy(node_grad, node_grad_hbm, out_sem.at[1])
    last_write.start()
    for x in (edge_x, back_x, rot_x, msg_x):
        x.sent()
    for copy in ghosts:
        copy.wait_send()
    write.wait()
    last_write.wait()


def shards(
    nodes,
    ghost_send,
    edge_src,
    edge_dst,
    wigner,
    envelope,
    w_zero,
    w_one_real,
    w_one_imag,
    w_two_real,
    w_two_imag,
    cotangent,
):
    flat = NODE * 32
    node_rows = jnp.transpose(nodes, (1, 2, 0)).reshape(flat, LANES)
    cot_rows = jnp.transpose(cotangent, (1, 2, 0)).reshape(flat, LANES)
    wig = jnp.transpose(wigner, (2, 1, 0))
    atoms = pltpu.VMEM((flat, LANES), BF16)
    ghost = pltpu.VMEM((TOP * 32, LANES), BF16)
    packed = pltpu.VMEM((4, WIDE // LANES, 32, LANES), BF16)
    weights = (w_zero, w_one_real, w_one_imag, w_two_real, w_two_imag)
    copies = 4 * 3 * len(CHUNKS)
    anywhere = pl.BlockSpec(memory_space=pltpu.HBM)
    vmem = pl.BlockSpec(memory_space=pltpu.VMEM)
    updated, node_grad = pl.pallas_call(
        layer,
        out_shape=[jax.ShapeDtypeStruct((flat, LANES), BF16)] * 2,
        in_specs=[anywhere] * 3 + [vmem] * 4 + [anywhere] * 5,
        out_specs=[anywhere] * 2,
        scratch_shapes=[atoms, atoms, pltpu.VMEM(wig.shape, BF16)]
        + [pltpu.VMEM(w.shape, BF16) for w in weights]
        + [ghost] * 8
        + [packed] * 8
        + [
            pltpu.VMEM((WIDE, LANES), F32),
            pltpu.VMEM((flat, LANES), F32),
            atoms,
            pltpu.VMEM((flat, LANES), F32),
            atoms,
            atoms,
            pltpu.SemaphoreType.DMA((8,)),
            pltpu.SemaphoreType.DMA((2,)),
            pltpu.SemaphoreType.DMA((copies,)),
            pltpu.SemaphoreType.DMA((copies,)),
            pltpu.SemaphoreType.DMA((4,)),
            pltpu.SemaphoreType.DMA((4,)),
        ],
        compiler_params=pltpu.CompilerParams(
            vmem_limit_bytes=60 * 1024 * 1024, collective_id=0, has_side_effects=True
        ),
    )(
        node_rows,
        cot_rows,
        wig,
        ghost_send.reshape(1, LANES),
        edge_src.reshape(1, LANES),
        edge_dst.reshape(1, LANES),
        envelope.reshape(1, LANES),
        *weights,
    )

    def restore(x):
        return jnp.transpose(x.reshape(NODE, 32, LANES), (2, 0, 1))

    return restore(updated), restore(node_grad)


def solution(mesh):
    in_specs = (
        P("space", None, "morder"),
        P("space"),
        P("space"),
        P("space"),
        P("space", None, None),
        P("space"),
        P(),
        P(),
        P(),
        P(),
        P(),
        P("space", None, "morder"),
    )
    out_specs = (P("space", None, "morder"), P("space", None, "morder"))
    return jax.shard_map(shards, mesh=mesh, in_specs=in_specs, out_specs=out_specs, check_vma=False)
```

time: 95.8 us -> 64.7 us (0.68)
  the two profiles are of different devices: /device:TPU:9 before, /device:TPU:263 now
where the time goes in v1:
time: 64.7 us; the launch traced here: 64.5 us
  Pallas kernels  60.3 us (93%)
  local copies, waits for them, and re-layouts  3.54 us (5%)
    pallas_call x1, Pallas kernels, shards(): pl.pallas_call(layer, out_shape=[jax.ShapeDtypeStruct((flat, LANES), BF16...  60.3 us
    unnamed x2, local copies, waits for them, and re-layouts  3.54 us

profile of v1, /device:TPU:263, one launch (start us, length us, event | category | flops | bytes accessed | tf_op | source)
XLA Modules:
  0.0 64.5 jit_solution(15776243485535419165)
XLA Ops:
  0.6 60.3 %shard_map.131 = (bf16[1568,128]{1,0:T(8,128)(2,1)}, bf16[1568,128]{1,0:T(8,128)(2,1)}) custom-call(bf16[1568,128]{1,0:T(8,128)(2,1)} %bitcast.17, bf16[1568,128]{1,0:T(8,128)(2,1)} %bitcast.18, bf16[49,29,128]{2,1,0:T(8,128)(2,1)} %bitcast.19, s32[1,128]{1,0:T(1,128)} %bitcast.22, s32[1,128]{1,0:T(1,128)} %bitcast.23, s32[1,128]{1,0:T(1,128)} %bitcast.24, ...), custom_call_target="tpu_custom_call" | custom-call | tf_op jit(solution)/shard_map/pallas_call | solution.py:443
  60.9 1.8 %copy.16 = bf16[128,49,32]{0,2,1:T(8,128)(2,1)} copy(bf16[128,49,32]{0,2,1:T(8,128)(2,1)} %bitcast.21) | data formatting | bytes 802816
  62.7 1.8 %copy.17 = bf16[128,49,32]{0,2,1:T(8,128)(2,1)} copy(bf16[128,49,32]{0,2,1:T(8,128)(2,1)} %bitcast.20) | data formatting | bytes 802816

commit v2 on v1

--- a/solution.py
+++ b/solution.py
@@ -7,11 +7,11 @@
 
 F32, BF16 = jnp.float32, jnp.bfloat16
 LANES = 128
-TOP = 25
+HALF = 784
 NODE = 49
 EDGE = 29
-WIDE = 1024
-PARTS = ((0, 7), (7, 6), (13, 6), (19, 5), (24, 5))
+PACKED = 240
+PARTS = ((0, 6), (6, 6), (12, 5), (17, 5), (22, 7))
 
 
 def degree_rows(degree):
@@ -63,6 +63,10 @@
                 term = rot_ref[n, k : k + 1, :].astype(F32) * load(k)
                 total = term if total is None else total + term
             store(n, total)
+
+
+def place(k):
+    return k - 7 if k >= 7 else k + 22
 
 
 def channel_rows(n, count=1):
@@ -84,32 +88,64 @@
     return [b0, b1, b2, b3]
 
 
-CHUNKS = ((0, 2), (2, 5), (5, 8))
+CHUNKS = ((0, 3), (3, 8))
+
+
+def span_of(group):
+    return slice(group * 32, min(group * 32 + 32, PACKED))
+
+
+def fold(block):
+    lane = lax.broadcasted_iota(jnp.int32, (16, LANES), 1)
+    return jnp.where(lane < 32, block[:16], pltpu.roll(block[16:], 32, 1))
+
+
+def unfold(block):
+    return jnp.concatenate([block, pltpu.roll(block, 96, 1)], 0)
 
 
 def store_transposed(rows_ref, out_ref, first, last):
     for group in range(first, last):
-        piece = rows_ref[group * LANES : (group + 1) * LANES, :].T.astype(BF16)
+        piece = rows_ref[group * LANES : (group + 1) * LANES, :].T
         for part in range(4):
-            out_ref[part, group] = piece[part * 32 : (part + 1) * 32]
+            block = piece[part * 32 : (part + 1) * 32]
+            if group == 7:
+                block = fold(block)
+            out_ref[part, span_of(group)] = block.astype(BF16)
+
+
+def load_group(in_ref, part, group):
+    block = in_ref[part, span_of(group)].astype(F32)
+    return unfold(block) if group == 7 else block
 
 
 def load_transposed(in_ref, rows_ref, first, last):
     for group in range(first, last):
-        piece = jnp.concatenate([in_ref[part, group].astype(F32) for part in range(4)], axis=0)
+        piece = jnp.concatenate([load_group(in_ref, part, group) for part in range(4)], axis=0)
         rows_ref[group * LANES : (group + 1) * LANES, :] = piece.T
 
 
+def piece_span(piece):
+    first, last = CHUNKS[piece]
+    return pl.ds(first * 32, min(last * 32, PACKED) - first * 32)
+
+
 class Exchange:
-    def __init__(self, send, recv, send_sem, recv_sem, base):
+    def __init__(self, send, recv, send_sem, recv_sem, base, kept_sem=None):
         self.send, self.recv = send, recv
         self.space, self.me = lax.axis_index("space"), lax.axis_index("morder")
         self.copies = {}
-        for piece, (first, last) in enumerate(CHUNKS):
+        self.kept = []
+        for piece in range(len(CHUNKS)):
+            if kept_sem is not None:
+                span = piece_span(piece)
+                self.kept.append(
+                    pltpu.make_async_copy(send.at[self.me, span], recv.at[self.me, span], kept_sem.at[piece])
+                )
             for step in (1, 2, 3):
                 target = lax.rem(self.me + step, 4)
                 slot = base + piece * 3 + step - 1
-                span = pl.ds(first, last - first)
+                span = piece_span(piece)
                 self.copies[piece, step] = pltpu.make_async_remote_copy(
                     src_ref=send.at[target, span],
                     dst_ref=recv.at[self.me, span],
@@ -122,20 +158,25 @@
     def start(self, piece):
         for step in (2, 1, 3):
             self.copies[piece, step].start()
-        first, last = CHUNKS[piece]
-        self.recv[self.me, first:last] = self.send[self.me, first:last]
+        if self.kept:
+            self.kept[piece].start()
+        else:
+            span = piece_span(piece)
+            self.recv[self.me, span] = self.send[self.me, span]
 
     def arrived(self, piece):
         for step in (1, 2, 3):
             self.copies[piece, step].wait_recv()
 
     def sent(self):
+        for copy in self.kept:
+            copy.wait()
         for copy in self.copies.values():
             copy.wait_send()
 
 
 def gather_group(in_ref, group):
-    return swap_blocks([in_ref[i, group].astype(F32) for i in range(4)])
+    return swap_blocks([load_group(in_ref, i, group) for i in range(4)])
 
 
 def map_edges(forward, before, after, weights):
@@ -169,31 +210,27 @@
     def give(piece):
         for group in range(*CHUNKS[piece]):
             for i, value in enumerate(swap_blocks(results[4 * group : 4 * group + 4])):
-                after.send[i, group] = value.astype(BF16)
+                if group == 7:
+                    value = fold(value)
+                after.send[i, span_of(group)] = value.astype(BF16)
         after.start(piece)
 
     take(0)
-    put(product(part(0), w_zero[...]))
+    pair(0, w_one_real, w_one_imag)
+    give(0)
     take(1)
-    pair(1, w_one_real, w_one_imag)
-    give(0)
-    take(2)
-    pair(3, w_two_real, w_two_imag)
+    pair(2, w_two_real, w_two_imag)
+    put(product(part(4), w_zero[...]))
+    results.extend([jnp.zeros_like(results[0])] * 3)
     give(1)
-    results.extend([jnp.zeros_like(results[0])] * 3)
-    give(2)
 
 
 def ghost_pack(product, source, first, second, low, high):
-    for n in range(0, TOP, 5):
-        both = product(source[channel_rows(n, 5)], first)
-        count = min(5, NODE - TOP - n)
-        other = product(source[channel_rows(TOP + n, count)], second)
-        if count < 5:
-            other = jnp.concatenate([other, jnp.zeros(((5 - count) * 32, 256), F32)], 0)
-        both = (both + other).astype(BF16)
-        low[channel_rows(n, 5)] = both[:, :LANES]
-        high[channel_rows(n, 5)] = both[:, LANES:]
+    for row in range(0, HALF, 112):
+        both = product(source[row : row + 112], first) + product(source[HALF + row : HALF + row + 112], second)
+        both = both.astype(BF16)
+        low[row : row + 112] = both[:, :LANES]
+        high[row : row + 112] = both[:, LANES:]
 
 
 def layer(
@@ -209,8 +246,10 @@
     w1i_hbm,
     w2r_hbm,
     w2i_hbm,
-    updated_hbm,
-    node_grad_hbm,
+    msg_recv,
+    own_hbm,
+    below_grad,
+    above_grad,
     nodes,
     cot,
     wig,
@@ -225,8 +264,6 @@
     above,
     low_grad,
     high_grad,
-    below_grad,
-    above_grad,
     edge_send,
     edge_recv,
     back_send,
@@ -234,15 +271,13 @@
     rot_send,
     rot_recv,
     msg_send,
-    msg_recv,
     rows,
     hot,
     hot_half,
     own_grad,
-    updated,
-    node_grad,
     local_sem,
     out_sem,
+    kept_sem,
     send_sem,
     recv_sem,
     ghost_send_sem,
@@ -295,24 +330,22 @@
     edge_x = Exchange(edge_send, edge_recv, send_sem, recv_sem, 0)
     back_x = Exchange(back_send, back_recv, send_sem, recv_sem, pieces)
     rot_x = Exchange(rot_send, rot_recv, send_sem, recv_sem, 2 * pieces)
-    msg_x = Exchange(msg_send, msg_recv, send_sem, recv_sem, 3 * pieces)
+    msg_x = Exchange(msg_send, msg_recv, send_sem, recv_sem, 3 * pieces, kept_sem)
 
     side, rside = lane_low(), row_low()
     zero = jnp.zeros((LANES, LANES), F32)
     scale = env_ref[...]
-    rows[EDGE * 32 :] = jnp.zeros((WIDE - EDGE * 32, LANES), F32)
-    split = TOP * 32
-    rest = (NODE - TOP) * 32
+    rows[EDGE * 32 :] = jnp.zeros((8 * LANES - EDGE * 32, LANES), F32)
 
     loads[0].wait()
     hot[...] = dot(cot[...], one_hot(dst_ref[...]).astype(BF16))
     loads[1].wait()
 
     def store_scaled(k, value):
-        rows[channel_rows(k)] = value * scale
+        rows[channel_rows(place(k))] = value * scale
 
     def store_plain(k, value):
-        rows[channel_rows(k)] = value
+        rows[channel_rows(place(k))] = value
 
     rotate(wig, lambda n: hot[channel_rows(n)], store_scaled)
     for piece, (first, last) in enumerate(CHUNKS):
@@ -321,6 +354,7 @@
             pl.semaphore_wait(barrier, len(peers))
         edge_x.start(piece)
 
+    edge_x.sent()
     match = one_hot(send_ref[...])
     turned = pltpu.roll(match, 64, 1)
     loads[2].wait()
@@ -347,11 +381,11 @@
 
     ghosts[0].wait_recv()
     ghosts[1].wait_recv()
-    hot[:split] += dot(below[...], jnp.where(rside, zero, down).astype(BF16)) + dot(
+    hot[:HALF] += dot(below[...], jnp.where(rside, zero, down).astype(BF16)) + dot(
         above[...], jnp.where(rside, up, zero).astype(BF16)
     )
-    hot[split:] += dot(below[:rest], jnp.where(rside, plain, zero).astype(BF16)) + dot(
-        above[:rest], jnp.where(rside, zero, plain).astype(BF16)
+    hot[HALF:] += dot(below[...], jnp.where(rside, plain, zero).astype(BF16)) + dot(
+        above[...], jnp.where(rside, zero, plain).astype(BF16)
     )
     rotate(wig, lambda n: hot[channel_rows(n)], store_plain)
     for piece, (first, last) in enumerate(CHUNKS):
@@ -365,7 +399,7 @@
     def store_half(n, value):
         hot_half[channel_rows(n)] = value.astype(BF16)
 
-    rotate_back(wig, lambda k: rows[channel_rows(k)], store_half)
+    rotate_back(wig, lambda k: rows[channel_rows(place(k))], store_half)
     ghost_pack(
         dot_t,
         hot_half,
@@ -377,42 +411,94 @@
     ghosts[2].start()
     ghosts[3].start()
     own_grad[...] = dot_t(hot_half[...], own) + cot[...].astype(F32)
+    last_write = pltpu.make_async_copy(own_grad, own_hbm, out_sem.at[0])
+    last_write.start()
 
     map_edges(True, rot_x, msg_x, weights)
 
-    for piece, (first, last) in enumerate(CHUNKS):
+    for piece in range(len(CHUNKS)):
         msg_x.arrived(piece)
-        load_transposed(msg_recv, rows, first, last)
-
-    def store_message(n, value):
-        hot_half[channel_rows(n)] = (value * scale).astype(BF16)
-
-    rotate_back(wig, lambda k: rows[channel_rows(k)], store_message)
-    total = dot_t(hot_half[...], one_hot(dst_ref[...]).astype(BF16))
-    updated[...] = (nodes[...].astype(F32) + total).astype(BF16)
-    write = pltpu.make_async_copy(updated, updated_hbm, out_sem.at[0])
-    write.start()
-
     ghosts[2].wait_recv()
     ghosts[3].wait_recv()
-    match = one_hot(send_ref[...])
-    turned = pltpu.roll(match, 64, 1)
-    top = dot_t(above_grad[...], jnp.where(side, turned, zero).astype(BF16)) + dot_t(
-        below_grad[...], jnp.where(side, zero, turned).astype(BF16)
-    )
-    node_grad[:split] = (own_grad[:split] + top).astype(BF16)
-    bottom = dot_t(above_grad[:rest], jnp.where(side, zero, match).astype(BF16)) + dot_t(
-        below_grad[:rest], jnp.where(side, match, zero).astype(BF16)
-    )
-    node_grad[split:] = (own_grad[split:] + bottom).astype(BF16)
-    last_write = pltpu.make_async_copy(node_grad, node_grad_hbm, out_sem.at[1])
-    last_write.start()
-    for x in (edge_x, back_x, rot_x, msg_x):
+    for x in (back_x, rot_x, msg_x):
         x.sent()
     for copy in ghosts:
         copy.wait_send()
-    write.wait()
     last_write.wait()
+
+
+def finish(
+    msg_hbm,
+    wig_hbm,
+    nodes_hbm,
+    own_hbm,
+    below_hbm,
+    above_hbm,
+    send_ref,
+    dst_ref,
+    env_ref,
+    updated_hbm,
+    grad_hbm,
+    msg,
+    wig,
+    nodes,
+    own,
+    below,
+    above,
+    rows,
+    hot,
+    updated,
+    grad,
+    sem,
+    out_sem,
+):
+    loads = [
+        pltpu.make_async_copy(a, b, sem.at[i])
+        for i, (a, b) in enumerate(
+            (
+                (msg_hbm, msg),
+                (wig_hbm, wig),
+                (nodes_hbm, nodes),
+                (above_hbm, above),
+                (below_hbm, below),
+                (own_hbm, own),
+            )
+        )
+    ]
+    for load in loads:
+        load.start()
+    match = one_hot(send_ref[...])
+    turned = pltpu.roll(match, 64, 1)
+    side = lane_low()
+    zero = jnp.zeros((LANES, LANES), F32)
+    pairs = (
+        (jnp.where(side, turned, zero), jnp.where(side, zero, turned)),
+        (jnp.where(side, zero, match), jnp.where(side, match, zero)),
+    )
+    target = one_hot(dst_ref[...]).astype(BF16)
+    scale = env_ref[...]
+    loads[0].wait()
+    load_transposed(msg, rows, 0, 8)
+    loads[1].wait()
+
+    def store_message(n, value):
+        hot[channel_rows(n)] = (value * scale).astype(BF16)
+
+    rotate_back(wig, lambda k: rows[channel_rows(place(k))], store_message)
+    loads[2].wait()
+    updated[...] = (nodes[...].astype(F32) + dot_t(hot[...], target)).astype(BF16)
+    writes = [pltpu.make_async_copy(updated, updated_hbm, out_sem.at[0])]
+    writes[0].start()
+    for load in loads[3:]:
+        load.wait()
+    for half, (for_above, for_below) in enumerate(pairs):
+        span = pl.ds(half * HALF, HALF)
+        total = dot_t(above[...], for_above.astype(BF16)) + dot_t(below[...], for_below.astype(BF16))
+        grad[span] = (own[span] + total).astype(BF16)
+        writes.append(pltpu.make_async_copy(grad.at[span], grad_hbm.at[span], out_sem.at[1 + half]))
+        writes[-1].start()
+    for write in writes:
+        write.wait()
 
 
 def shards(
@@ -434,30 +520,35 @@
     cot_rows = jnp.transpose(cotangent, (1, 2, 0)).reshape(flat, LANES)
     wig = jnp.transpose(wigner, (2, 1, 0))
     atoms = pltpu.VMEM((flat, LANES), BF16)
-    ghost = pltpu.VMEM((TOP * 32, LANES), BF16)
-    packed = pltpu.VMEM((4, WIDE // LANES, 32, LANES), BF16)
+    ghost = pltpu.VMEM((HALF, LANES), BF16)
+    packed = pltpu.VMEM((4, PACKED, LANES), BF16)
     weights = (w_zero, w_one_real, w_one_imag, w_two_real, w_two_imag)
     copies = 4 * 3 * len(CHUNKS)
     anywhere = pl.BlockSpec(memory_space=pltpu.HBM)
     vmem = pl.BlockSpec(memory_space=pltpu.VMEM)
-    updated, node_grad = pl.pallas_call(
+    rows16 = jax.ShapeDtypeStruct((flat, LANES), BF16)
+    rows32 = jax.ShapeDtypeStruct((flat, LANES), F32)
+    returned = jax.ShapeDtypeStruct((HALF, LANES), BF16)
+    send = ghost_send.reshape(1, LANES)
+    dst = edge_dst.reshape(1, LANES)
+    env = envelope.reshape(1, LANES)
+    message, own_grad, below_grad, above_grad = pl.pallas_call(
         layer,
-        out_shape=[jax.ShapeDtypeStruct((flat, LANES), BF16)] * 2,
+        out_shape=[jax.ShapeDtypeStruct((4, PACKED, LANES), BF16), rows32, returned, returned],
         in_specs=[anywhere] * 3 + [vmem] * 4 + [anywhere] * 5,
-        out_specs=[anywhere] * 2,
+        out_specs=[anywhere] * 4,
         scratch_shapes=[atoms, atoms, pltpu.VMEM(wig.shape, BF16)]
         + [pltpu.VMEM(w.shape, BF16) for w in weights]
-        + [ghost] * 8
-        + [packed] * 8
+        + [ghost] * 6
+        + [packed] * 7
         + [
-            pltpu.VMEM((WIDE, LANES), F32),
+            pltpu.VMEM((8 * LANES, LANES), F32),
             pltpu.VMEM((flat, LANES), F32),
             atoms,
             pltpu.VMEM((flat, LANES), F32),
-            atoms,
-            atoms,
             pltpu.SemaphoreType.DMA((8,)),
-            pltpu.SemaphoreType.DMA((2,)),
+            pltpu.SemaphoreType.DMA((1,)),
+            pltpu.SemaphoreType.DMA((len(CHUNKS),)),
             pltpu.SemaphoreType.DMA((copies,)),
             pltpu.SemaphoreType.DMA((copies,)),
             pltpu.SemaphoreType.DMA((4,)),
@@ -470,12 +561,33 @@
         node_rows,
         cot_rows,
         wig,
-        ghost_send.reshape(1, LANES),
+        send,
         edge_src.reshape(1, LANES),
-        edge_dst.reshape(1, LANES),
-        envelope.reshape(1, LANES),
+        dst,
+        env,
         *weights,
     )
+    updated, node_grad = pl.pallas_call(
+        finish,
+        out_shape=[rows16, rows16],
+        in_specs=[anywhere] * 6 + [vmem] * 3,
+        out_specs=[anywhere] * 2,
+        scratch_shapes=[
+            packed,
+            pltpu.VMEM(wig.shape, BF16),
+            atoms,
+            pltpu.VMEM((flat, LANES), F32),
+            ghost,
+            ghost,
+            pltpu.VMEM((8 * LANES, LANES), F32),
+            atoms,
+            atoms,
+            atoms,
+            pltpu.SemaphoreType.DMA((6,)),
+            pltpu.SemaphoreType.DMA((3,)),
+        ],
+        compiler_params=pltpu.CompilerParams(vmem_limit_bytes=60 * 1024 * 1024),
+    )(message, wig, node_rows, own_grad, below_grad, above_grad, send, dst, env)
 
     def restore(x):
         return jnp.transpose(x.reshape(NODE, 32, LANES), (2, 0, 1))

time: 64.7 us -> 58.9 us (0.910)
  the two profiles are of different devices: /device:TPU:263 before, /device:TPU:8 now
where the time goes in v2:
time: 58.9 us; the launch traced here: 58.7 us
  Pallas kernels  58 us (98%)
  between operations  0.64 us (1%)
    pallas_call x1, Pallas kernels, shards(): pl.pallas_call(layer, out_shape=[jax.ShapeDtypeStruct((4, PACKED, LANES),...  54.3 us
    pallas_call x1, Pallas kernels, shards(): pl.pallas_call(finish, out_shape=[rows16, rows16], in_specs=[anywhere] *...  3.76 us

profile of v2, /device:TPU:8, one launch (start us, length us, event | category | flops | bytes accessed | tf_op | source)
XLA Modules:
  0.0 58.7 jit_solution(8103453120790368941)
XLA Ops:
  0.6 54.3 %shard_map.131 = (bf16[4,240,128]{2,1,0:T(8,128)(2,1)}, f32[1568,128]{1,0:T(8,128)}, bf16[784,128]{1,0:T(8,128)(2,1)}, bf16[784,128]{1,0:T(8,128)(2,1)}) custom-call(bf16[1568,128]{1,0:T(8,128)(2,1)} %bitcast.17, bf16[1568,128]{1,0:T(8,128)(2,1)} %bitcast.21, bf16[49,29,128]{2,1,0:T(8,128)(2,1)} %bitcast.19, s32[1,128]{1,0:T(1,128)} %bitcast.22, ...), custom_call_target="tpu_custom_call" | custom-call | tf_op jit(solution)/shard_map/pallas_call | solution.py:535
  54.9 3.8 %shard_map.132 = (bf16[1568,128]{1,0:T(8,128)(2,1)}, bf16[1568,128]{1,0:T(8,128)(2,1)}) custom-call(bf16[4,240,128]{2,1,0:T(8,128)(2,1)} %get-tuple-element.8.msg_hbm, bf16[49,29,128]{2,1,0:T(8,128)(2,1)} %bitcast.20, bf16[1568,128]{1,0:T(8,128)(2,1)} %bitcast.18, f32[1568,128]{1,0:T(8,128)} %get-tuple-element.9.own_hbm, ...), custom_call_target="tpu_custom_call" | custom-call | tf_op jit(solution)/shard_map/pallas_call | solution.py:570

commit v3 on v2

--- a/solution.py
+++ b/solution.py
@@ -44,10 +44,16 @@
     return lax.broadcasted_iota(jnp.int32, (LANES, LANES), 0) < LANES // 2
 
 
-def rotate(rot_ref, load, store):
+FIRST_ROWS = range(7, 19)
+LATER_ROWS = tuple(range(19, 29)) + tuple(range(7))
+
+
+def rotate(rot_ref, load, store, wanted):
     for degree in range(7):
         columns = range(degree * degree, (degree + 1) * (degree + 1))
         for k in degree_rows(degree):
+            if k not in wanted:
+                continue
             total = None
             for n in columns:
                 term = rot_ref[n, k : k + 1, :].astype(F32) * load(n)
@@ -175,11 +181,11 @@
             copy.wait_send()
 
 
-def gather_group(in_ref, group):
-    return swap_blocks([load_group(in_ref, i, group) for i in range(4)])
-
-
-def map_edges(forward, before, after, weights):
+def mirrored(blocks, far):
+    return [jnp.where(far, blocks[3 - i], blocks[i]) for i in range(4)]
+
+
+def map_edges(forward, before, after, weights, far):
     w_zero, w_one_real, w_one_imag, w_two_real, w_two_imag = weights
     product = dot if forward else dot_t
     blocks, results = [], []
@@ -187,7 +193,8 @@
     def take(piece):
         before.arrived(piece)
         for group in range(*CHUNKS[piece]):
-            blocks.extend(gather_group(before.recv, group))
+            parts = [load_group(before.recv, i, group) for i in range(4)]
+            blocks.extend(swap_blocks(mirrored(parts, far) if forward else parts))
 
     def part(i):
         start, count = PARTS[i]
@@ -209,7 +216,8 @@
 
     def give(piece):
         for group in range(*CHUNKS[piece]):
-            for i, value in enumerate(swap_blocks(results[4 * group : 4 * group + 4])):
+            parts = swap_blocks(results[4 * group : 4 * group + 4])
+            for i, value in enumerate(parts if forward else mirrored(parts, far)):
                 if group == 7:
                     value = fold(value)
                 after.send[i, span_of(group)] = value.astype(BF16)
@@ -275,6 +283,7 @@
     hot,
     hot_half,
     own_grad,
+    far_rows,
     local_sem,
     out_sem,
     kept_sem,
@@ -287,7 +296,11 @@
     domains = lax.axis_size("space")
     upper = lax.rem(space + 1, domains)
     lower = lax.rem(space + domains - 1, domains)
-    peers = [(upper, me), (lower, me)] + [(space, lax.rem(me + step, 4)) for step in (1, 2, 3)]
+    odd = lax.rem(space, 2)
+    mirror = 3 - 2 * me
+    upper_place = me + odd * mirror
+    lower_place = me + (1 - odd) * mirror
+    peers = [(upper, upper_place), (lower, lower_place)] + [(space, lax.rem(me + step, 4)) for step in (1, 2, 3)]
     barrier = pltpu.get_barrier_semaphore()
     for peer in peers:
         pl.semaphore_signal(barrier, inc=1, device_id=peer, device_id_type=pl.DeviceIdType.MESH)
@@ -310,21 +323,21 @@
         load.start()
     weights = (w0, w1r, w1i, w2r, w2i)
 
-    def ghost_copy(slot, source, target, device):
+    def ghost_copy(slot, source, target, device, position):
         return pltpu.make_async_remote_copy(
             src_ref=source,
             dst_ref=target,
             send_sem=ghost_send_sem.at[slot],
             recv_sem=ghost_recv_sem.at[slot],
-            device_id=(device, me),
+            device_id=(device, position),
             device_id_type=pl.DeviceIdType.MESH,
         )
 
     ghosts = [
-        ghost_copy(0, high, below, upper),
-        ghost_copy(1, low, above, lower),
-        ghost_copy(2, high_grad, below_grad, upper),
-        ghost_copy(3, low_grad, above_grad, lower),
+        ghost_copy(0, high, below, upper, upper_place),
+        ghost_copy(1, low, above, lower, lower_place),
+        ghost_copy(2, high_grad, below_grad, upper, upper_place),
+        ghost_copy(3, low_grad, above_grad, lower, lower_place),
     ]
     pieces = len(CHUNKS) * 3
     edge_x = Exchange(edge_send, edge_recv, send_sem, recv_sem, 0)
@@ -347,14 +360,13 @@
     def store_plain(k, value):
         rows[channel_rows(place(k))] = value
 
-    rotate(wig, lambda n: hot[channel_rows(n)], store_scaled)
     for piece, (first, last) in enumerate(CHUNKS):
+        rotate(wig, lambda n: hot[channel_rows(n)], store_scaled, (FIRST_ROWS, LATER_ROWS)[piece])
         store_transposed(rows, edge_send, first, last)
         if piece == 0:
             pl.semaphore_wait(barrier, len(peers))
         edge_x.start(piece)
 
-    edge_x.sent()
     match = one_hot(send_ref[...])
     turned = pltpu.roll(match, 64, 1)
     loads[2].wait()
@@ -377,7 +389,11 @@
 
     for load in loads[3:]:
         load.wait()
-    map_edges(False, edge_x, back_x, weights)
+    first_far = LANES + 64 * odd
+    is_far = jnp.where((index >= first_far) & (index < first_far + 64), 1.0, 0.0).astype(F32)
+    far_rows[...] = jnp.broadcast_to(is_far, (LANES, LANES)).T
+    far = far_rows[pl.ds(pl.multiple_of(me * 32, 32), 32)] > 0.5
+    map_edges(False, edge_x, back_x, weights, far)
 
     ghosts[0].wait_recv()
     ghosts[1].wait_recv()
@@ -387,8 +403,8 @@
     hot[HALF:] += dot(below[...], jnp.where(rside, plain, zero).astype(BF16)) + dot(
         above[...], jnp.where(rside, zero, plain).astype(BF16)
     )
-    rotate(wig, lambda n: hot[channel_rows(n)], store_plain)
     for piece, (first, last) in enumerate(CHUNKS):
+        rotate(wig, lambda n: hot[channel_rows(n)], store_plain, (FIRST_ROWS, LATER_ROWS)[piece])
         store_transposed(rows, rot_send, first, last)
         rot_x.start(piece)
 
@@ -414,13 +430,13 @@
     last_write = pltpu.make_async_copy(own_grad, own_hbm, out_sem.at[0])
     last_write.start()
 
-    map_edges(True, rot_x, msg_x, weights)
+    map_edges(True, rot_x, msg_x, weights, far_rows[pl.ds(pl.multiple_of(me * 32, 32), 32)] > 0.5)
 
     for piece in range(len(CHUNKS)):
         msg_x.arrived(piece)
     ghosts[2].wait_recv()
     ghosts[3].wait_recv()
-    for x in (back_x, rot_x, msg_x):
+    for x in (edge_x, back_x, rot_x, msg_x):
         x.sent()
     for copy in ghosts:
         copy.wait_send()
@@ -546,6 +562,7 @@
             pltpu.VMEM((flat, LANES), F32),
             atoms,
             pltpu.VMEM((flat, LANES), F32),
+            pltpu.VMEM((LANES, LANES), F32),
             pltpu.SemaphoreType.DMA((8,)),
             pltpu.SemaphoreType.DMA((1,)),
             pltpu.SemaphoreType.DMA((len(CHUNKS),)),

time: 58.9 us -> 49.1 us (0.83)
  Pallas kernels: 58 us -> 48.2 us
    pallas_call x1, Pallas kernels: 54.3 us -> 44.5 us  [shards(): pl.pallas_call(layer, out_shape=[jax.ShapeDtypeStruct((4, PACKED, LANES),...]
where the time goes in v3:
time: 49.1 us; the launch traced here: 48.9 us
  Pallas kernels  48.2 us (98%)
  between operations  0.64 us (1%)
    pallas_call x1, Pallas kernels, shards(): pl.pallas_call(layer, out_shape=[jax.ShapeDtypeStruct((4, PACKED, LANES),...  44.5 us
    pallas_call x1, Pallas kernels, shards(): pl.pallas_call(finish, out_shape=[rows16, rows16], in_specs=[anywhere] *...  3.75 us

profile of v3, /device:TPU:8, one launch (start us, length us, event | category | flops | bytes accessed | tf_op | source)
XLA Modules:
  0.0 48.9 jit_solution(16446732188751082878)
XLA Ops:
  0.6 44.5 %shard_map.131 = (bf16[4,240,128]{2,1,0:T(8,128)(2,1)}, f32[1568,128]{1,0:T(8,128)}, bf16[784,128]{1,0:T(8,128)(2,1)}, bf16[784,128]{1,0:T(8,128)(2,1)}) custom-call(bf16[1568,128]{1,0:T(8,128)(2,1)} %bitcast.17, bf16[1568,128]{1,0:T(8,128)(2,1)} %bitcast.21, bf16[49,29,128]{2,1,0:T(8,128)(2,1)} %bitcast.19, s32[1,128]{1,0:T(1,128)} %bitcast.22, ...), custom_call_target="tpu_custom_call" | custom-call | tf_op jit(solution)/shard_map/pallas_call | solution.py:551
  45.1 3.8 %shard_map.132 = (bf16[1568,128]{1,0:T(8,128)(2,1)}, bf16[1568,128]{1,0:T(8,128)(2,1)}) custom-call(bf16[4,240,128]{2,1,0:T(8,128)(2,1)} %get-tuple-element.8.msg_hbm, bf16[49,29,128]{2,1,0:T(8,128)(2,1)} %bitcast.20, bf16[1568,128]{1,0:T(8,128)(2,1)} %bitcast.18, f32[1568,128]{1,0:T(8,128)} %get-tuple-element.9.own_hbm, ...), custom_call_target="tpu_custom_call" | custom-call | tf_op jit(solution)/shard_map/pallas_call | solution.py:587

commit v4 on v3

--- a/solution.py
+++ b/solution.py
@@ -319,7 +319,7 @@
             )
         )
     ]
-    for load in loads:
+    for load in loads[:3]:
         load.start()
     weights = (w0, w1r, w1i, w2r, w2i)
 
@@ -353,33 +353,39 @@
     loads[0].wait()
     hot[...] = dot(cot[...], one_hot(dst_ref[...]).astype(BF16))
     loads[1].wait()
+    for load in loads[3:]:
+        load.start()
 
     def store_scaled(k, value):
         rows[channel_rows(place(k))] = value * scale
 
     def store_plain(k, value):
         rows[channel_rows(place(k))] = value
+
+    def pack():
+        match = one_hot(send_ref[...])
+        turned = pltpu.roll(match, 64, 1)
+        ghost_pack(
+            dot,
+            nodes,
+            jnp.concatenate([jnp.where(side, match, zero), jnp.where(side, zero, match)], 1).astype(BF16),
+            jnp.concatenate([jnp.where(side, zero, turned), jnp.where(side, turned, zero)], 1).astype(BF16),
+            low,
+            high,
+        )
 
     for piece, (first, last) in enumerate(CHUNKS):
         rotate(wig, lambda n: hot[channel_rows(n)], store_scaled, (FIRST_ROWS, LATER_ROWS)[piece])
         store_transposed(rows, edge_send, first, last)
         if piece == 0:
+            loads[2].wait()
+            pack()
             pl.semaphore_wait(barrier, len(peers))
         edge_x.start(piece)
-
-    match = one_hot(send_ref[...])
-    turned = pltpu.roll(match, 64, 1)
-    loads[2].wait()
-    ghost_pack(
-        dot,
-        nodes,
-        jnp.concatenate([jnp.where(side, match, zero), jnp.where(side, zero, match)], 1).astype(BF16),
-        jnp.concatenate([jnp.where(side, zero, turned), jnp.where(side, turned, zero)], 1).astype(BF16),
-        low,
-        high,
-    )
-    ghosts[0].start()
-    ghosts[1].start()
+        if piece == 0:
+            ghosts[0].start()
+            ghosts[1].start()
+
     index = src_ref[...]
     own = one_hot(index).astype(BF16)
     plain = one_hot(index, LANES)

time: 49.1 us -> 47.6 us (0.969)
  the two profiles are of different devices: /device:TPU:8 before, /device:TPU:6 now
where the time goes in v4:
time: 47.6 us; the launch traced here: 47.4 us
  Pallas kernels  46.8 us (98%)
  between operations  0.64 us (1%)
    pallas_call x1, Pallas kernels, shards(): pl.pallas_call(layer, out_shape=[jax.ShapeDtypeStruct((4, PACKED, LANES),...  43 us
    pallas_call x1, Pallas kernels, shards(): pl.pallas_call(finish, out_shape=[rows16, rows16], in_specs=[anywhere] *...  3.75 us

profile of v4, /device:TPU:6, one launch (start us, length us, event | category | flops | bytes accessed | tf_op | source)
XLA Modules:
  0.0 47.4 jit_solution(7261114362398499421)
XLA Ops:
  0.6 43.0 %shard_map.131 = (bf16[4,240,128]{2,1,0:T(8,128)(2,1)}, f32[1568,128]{1,0:T(8,128)}, bf16[784,128]{1,0:T(8,128)(2,1)}, bf16[784,128]{1,0:T(8,128)(2,1)}) custom-call(bf16[1568,128]{1,0:T(8,128)(2,1)} %bitcast.17, bf16[1568,128]{1,0:T(8,128)(2,1)} %bitcast.21, bf16[49,29,128]{2,1,0:T(8,128)(2,1)} %bitcast.19, s32[1,128]{1,0:T(1,128)} %bitcast.22, ...), custom_call_target="tpu_custom_call" | custom-call | tf_op jit(solution)/shard_map/pallas_call | solution.py:557
  43.7 3.8 %shard_map.132 = (bf16[1568,128]{1,0:T(8,128)(2,1)}, bf16[1568,128]{1,0:T(8,128)(2,1)}) custom-call(bf16[4,240,128]{2,1,0:T(8,128)(2,1)} %get-tuple-element.8.msg_hbm, bf16[49,29,128]{2,1,0:T(8,128)(2,1)} %bitcast.20, bf16[1568,128]{1,0:T(8,128)(2,1)} %bitcast.18, f32[1568,128]{1,0:T(8,128)} %get-tuple-element.9.own_hbm, ...), custom_call_target="tpu_custom_call" | custom-call | tf_op jit(solution)/shard_map/pallas_call | solution.py:593

commit v5 on v4

--- a/solution.py
+++ b/solution.py
@@ -377,14 +377,13 @@
     for piece, (first, last) in enumerate(CHUNKS):
         rotate(wig, lambda n: hot[channel_rows(n)], store_scaled, (FIRST_ROWS, LATER_ROWS)[piece])
         store_transposed(rows, edge_send, first, last)
-        if piece == 0:
-            loads[2].wait()
-            pack()
-            pl.semaphore_wait(barrier, len(peers))
-        edge_x.start(piece)
-        if piece == 0:
-            ghosts[0].start()
-            ghosts[1].start()
+    loads[2].wait()
+    pack()
+    pl.semaphore_wait(barrier, len(peers))
+    edge_x.start(0)
+    ghosts[0].start()
+    ghosts[1].start()
+    edge_x.start(1)
 
     index = src_ref[...]
     own = one_hot(index).astype(BF16)

time: 47.6 us -> 47.5 us (level)
  the two profiles are of different devices: /device:TPU:6 before, /device:TPU:2 now
where the time goes in v5:
time: 47.5 us; the launch traced here: 47.3 us
  Pallas kernels  46.7 us (98%)
  between operations  0.64 us (1%)
    pallas_call x1, Pallas kernels, shards(): pl.pallas_call(layer, out_shape=[jax.ShapeDtypeStruct((4, PACKED, LANES),...  42.9 us
    pallas_call x1, Pallas kernels, shards(): pl.pallas_call(finish, out_shape=[rows16, rows16], in_specs=[anywhere] *...  3.76 us

profile of v5, /device:TPU:2, one launch (start us, length us, event | category | flops | bytes accessed | tf_op | source)
XLA Modules:
  0.0 47.3 jit_solution(2277783181626452018)
XLA Ops:
  0.6 42.9 %shard_map.131 = (bf16[4,240,128]{2,1,0:T(8,128)(2,1)}, f32[1568,128]{1,0:T(8,128)}, bf16[784,128]{1,0:T(8,128)(2,1)}, bf16[784,128]{1,0:T(8,128)(2,1)}) custom-call(bf16[1568,128]{1,0:T(8,128)(2,1)} %bitcast.17, bf16[1568,128]{1,0:T(8,128)(2,1)} %bitcast.21, bf16[49,29,128]{2,1,0:T(8,128)(2,1)} %bitcast.19, s32[1,128]{1,0:T(1,128)} %bitcast.22, ...), custom_call_target="tpu_custom_call" | custom-call | tf_op jit(solution)/shard_map/pallas_call | solution.py:556
  43.5 3.8 %shard_map.132 = (bf16[1568,128]{1,0:T(8,128)(2,1)}, bf16[1568,128]{1,0:T(8,128)(2,1)}) custom-call(bf16[4,240,128]{2,1,0:T(8,128)(2,1)} %get-tuple-element.8.msg_hbm, bf16[49,29,128]{2,1,0:T(8,128)(2,1)} %bitcast.20, bf16[1568,128]{1,0:T(8,128)(2,1)} %bitcast.18, f32[1568,128]{1,0:T(8,128)} %get-tuple-element.9.own_hbm, ...), custom_call_target="tpu_custom_call" | custom-call | tf_op jit(solution)/shard_map/pallas_call | solution.py:592
